TPU v7x, 256 devices: a whole 4x4x8 slice. The times are simulated.
256 devices in a mesh: dp: 16 (over z_lo, x, core), cp: 16 (over y, z_hi).
Axes of the slice: x: 4, y: 4, z: 8 (z_hi: 4, z_lo: 2; z = z_hi * 2 + z_lo), core: 2. Of those that a mesh axis runs over, the one named last changes fastest.
Arguments:
- queries: bfloat16 [65536, 4096], P(('dp', 'cp')), may hold values from -128 to 128
- keys: bfloat16 [65536, 1024], P(('dp', 'cp')), may hold values from -6 to 6
- values: bfloat16 [65536, 1024], P(('dp', 'cp')), may hold values from -6 to 6
- grad_out: bfloat16 [65536, 4096], P(('dp', 'cp')), may hold values from -6 to 6
- segment_ids: int32 [65536], replicated, may hold values from 0 to 169, never falling along the last dimension, each value on 1 to 768 neighbouring positions
Outputs:
- attended: bfloat16 [65536, 4096], P(('dp', 'cp'))
- grad_queries: bfloat16 [65536, 4096], P(('dp', 'cp'))
- grad_keys: bfloat16 [65536, 1024], P(('dp', 'cp'))
- grad_values: bfloat16 [65536, 1024], P(('dp', 'cp'))
Inputs may be any that keep to these rules, and one draw needn't show every extreme that they name: `segment_ids`: document ids never fall along the packed tokens; each document holds 1 to 768 tokens and one holds exactly 768.
All inputs are finite; a program needn't handle non-finite values.
Results may differ from a plain program's by a relative error of at most 0.018.
Values may be sent and summed in bfloat16 or wider, within the bound.
No kernel may reach another device: no remote copies, remote signals or barrier semaphores. Data moves between devices by JAX's collectives and lax.ppermute only.
A program may use at most 128 MiB of HBM per device.

v0:
```python
import functools

import jax
import jax.numpy as jnp
from jax import lax
from jax.experimental import pallas as pl
from jax.experimental.pallas import tpu as pltpu
from jax.sharding import PartitionSpec as P

HQ = 32
HK = 8
HD = 128
GROUP = HQ // HK
REACH = 3
BLOCKS = REACH + 1
AXES = ("dp", "cp")
LOG2E = 1.4426950408889634
HIDDEN = -1e30

GROUPS = ((0, 4), (4, 4))
CALLS = ((0, 0, 2), (0, 2, 2), (1, 0, 2), (1, 2, 2))


def moved(value, steps):
    count = lax.axis_size(AXES)
    return lax.ppermute(value, AXES, [(i, (i + steps) % count) for i in range(count)])


def after(value, gate):
    return lax.optimization_barrier((value, gate))[0]


def dot_nt(a, b):
    return lax.dot_general(a, b, (((1,), (1,)), ((), ())), preferred_element_type=jnp.float32)


def dot_nn(a, b):
    return jnp.dot(a, b, preferred_element_type=jnp.float32)


def attend_kernel(split, total, seg_col, seg_row, q, do, *refs):
    *outs, bias, kcat, vcat, scores, ph, ds = refs[2 * BLOCKS :]
    outs = outs[-(5 + (split > 0) + (split < total)) :]
    att, dq, own, keep, back1, *sent = outs
    rows = q.shape[0]
    scale = HD**-0.5

    @pl.when(pl.program_id(0) == 0)
    def _():
        for b in range(BLOCKS):
            at = (REACH - b) * rows
            seen = seg_col[...] == seg_row[:, at : at + rows]
            if b == 0:
                key_pos = lax.broadcasted_iota(jnp.int32, seen.shape, 1)
                seen &= key_pos <= lax.broadcasted_iota(jnp.int32, seen.shape, 0)
            bias[:, b * rows : (b + 1) * rows] = jnp.where(seen, 0.0, HIDDEN)

    for b in range(BLOCKS):
        kcat[b * rows : (b + 1) * rows, :] = refs[2 * b][...]
        vcat[b * rows : (b + 1) * rows, :] = refs[2 * b + 1][...]

    def score(g):
        qg = q[:, g * HD : (g + 1) * HD]
        scores[g % 2] = dot_nt(qg, kcat[...]) * (scale * LOG2E) + bias[...]

    def exponent(g):
        t = scores[g % 2]
        e = jnp.exp2(t - jnp.max(t, axis=1, keepdims=True))
        ph[g % 2] = e.astype(jnp.bfloat16)
        return 1.0 / jnp.sum(e, axis=1, keepdims=True)

    dk = dv = None
    score(0)
    inv = exponent(0)
    for g in range(GROUP):
        cols = slice(g * HD, (g + 1) * HD)
        if g + 1 < GROUP:
            score(g + 1)
        out = (dot_nn(ph[g % 2], vcat[...]) * inv).astype(jnp.bfloat16)
        att[:, cols] = out
        dog = (do[:, cols].astype(jnp.float32) * inv).astype(jnp.bfloat16)
        delta = jnp.sum(dog.astype(jnp.float32) * out.astype(jnp.float32), axis=1, keepdims=True)
        dp = dot_nt(dog, vcat[...])
        ds[g % 2] = (ph[g % 2].astype(jnp.float32) * (dp - delta)).astype(jnp.bfloat16)
        if g + 1 < GROUP:
            inv = exponent(g + 1)
        dq[:, cols] = (dot_nn(ds[g % 2], kcat[...]) * scale).astype(jnp.bfloat16)
        a, c = dot_nn(q[:, cols].T, ds[g % 2]), dot_nn(dog.T, ph[g % 2])
        dk = a if g == 0 else dk + a
        dv = c if g == 0 else dv + c

    def put(ref, b):
        at = slice(b * rows, (b + 1) * rows)
        ref[0, 0] = (dk[:, at] * scale).T.astype(ref.dtype)
        ref[0, 1] = dv[:, at].T.astype(ref.dtype)

    put(own, 0)

    def put_low():
        put(back1, 2)
        put(sent[0], 3)
        put(keep, 1)

    def put_high():
        put(back1, 1)
        put(sent[-1], 2)
        put(keep, 3)

    if split == total:
        put_low()
    elif split == 0:
        put_high()
    else:
        pl.when(pl.program_id(0) < split)(put_low)
        pl.when(pl.program_id(0) >= split)(put_high)


def attend(first, heads, split, seg_col, seg_row, q, do, k, v, received, prev):
    rows = q.shape[0]
    whole = lambda a: pl.BlockSpec(a.shape, lambda h: (0,) * a.ndim)
    wide = pl.BlockSpec((rows, GROUP * HD), lambda h: (0, first + h))
    own = pl.BlockSpec((rows, HD), lambda h: (0, first + h))
    in_specs = [whole(seg_col), whole(seg_row), wide, wide, own, own]
    args = [seg_col, seg_row, q, do, k, v]
    for block, at in received:
        for part in range(2):
            in_specs.append(
                pl.BlockSpec((None, rows, HD), lambda h, at=at, part=part: (part, 0, at + h))
            )
            args.append(block)
    aliases = {}
    if prev is not None:
        aliases = {len(args): 0, len(args) + 1: 1}
        in_specs += [pl.BlockSpec(memory_space=pl.ANY)] * 2
        args += list(prev)
    shape = (1, 2, rows, HD)
    each = pl.BlockSpec(shape, lambda h: (h, 0, 0, 0))
    specs, counts = [each] * 3, [heads] * 3
    if split > 0:
        specs.append(pl.BlockSpec(shape, lambda h: (jnp.minimum(h, split - 1), 0, 0, 0)))
        counts.append(split)
    if split < heads:
        specs.append(pl.BlockSpec(shape, lambda h: (jnp.maximum(h - split, 0), 0, 0, 0)))
        counts.append(heads - split)
    flops = 6 * 2 * rows * rows * BLOCKS * HD * GROUP * heads
    return pl.pallas_call(
        functools.partial(attend_kernel, split, heads),
        grid=(heads,),
        in_specs=in_specs,
        out_specs=[wide, wide] + specs,
        out_shape=[jax.ShapeDtypeStruct(q.shape, q.dtype)] * 2
        + [
            jax.ShapeDtypeStruct((n, 2, rows, HD), jnp.bfloat16 if i else jnp.float32)
            for i, n in enumerate(counts)
        ],
        scratch_shapes=[
            pltpu.VMEM((rows, BLOCKS * rows), jnp.float32),
            pltpu.VMEM((BLOCKS * rows, HD), jnp.bfloat16),
            pltpu.VMEM((BLOCKS * rows, HD), jnp.bfloat16),
            pltpu.VMEM((2, rows, BLOCKS * rows), jnp.float32),
            pltpu.VMEM((2, rows, BLOCKS * rows), jnp.bfloat16),
            pltpu.VMEM((2, rows, BLOCKS * rows), jnp.bfloat16),
        ],
        input_output_aliases=aliases,
        compiler_params=pltpu.CompilerParams(vmem_limit_bytes=48 * 1024 * 1024),
        cost_estimate=pl.CostEstimate(
            flops=flops, bytes_accessed=8 * 2**20, transcendentals=rows * rows * 4 * GROUP * heads
        ),
        name="attend",
    )(*args)


def finish_kernel(own, a, b, *refs):
    for part, ref in enumerate(refs[-2:]):
        for h in range(own.shape[0]):
            total = own[h, part] + a[h, part].astype(jnp.float32) + b[h, part].astype(jnp.float32)
            ref[:, h * HD : (h + 1) * HD] = total.astype(jnp.bfloat16)


def finish(first, heads, terms, prev):
    rows = terms[0][0].shape[2]
    unit = 2 if all(x % 2 == 0 for x in (first, heads, *[at for _, at in terms])) else 1
    specs = [
        pl.BlockSpec((unit, 2, rows, HD), lambda i, at=at: (at // unit + i, 0, 0, 0))
        for _, at in terms
    ]
    args, aliases = [t for t, _ in terms], {}
    out = pl.BlockSpec((rows, unit * HD), lambda i: (0, first // unit + i))
    if prev is not None:
        aliases = {3: 0, 4: 1}
        specs = specs + [pl.BlockSpec(memory_space=pl.ANY)] * 2
        args += list(prev)
    return pl.pallas_call(
        finish_kernel,
        grid=(heads // unit,),
        in_specs=specs,
        out_specs=[out, out],
        out_shape=[jax.ShapeDtypeStruct((rows, HK * HD), jnp.bfloat16)] * 2,
        input_output_aliases=aliases,
        cost_estimate=pl.CostEstimate(flops=10**6, bytes_accessed=3 * 2**20, transcendentals=0),
        name="finish",
    )(*args)


def shards(queries, keys, values, grad_out, segment_ids):
    rows = queries.shape[0]
    margin = REACH * rows
    first_row = lax.axis_index(AXES) * rows
    seg_pad = jnp.concatenate([jnp.full((margin,), -1, jnp.int32), segment_ids], 0)
    seg_row = lax.dynamic_slice_in_dim(seg_pad, first_row, margin + rows, 0)
    seg_col = seg_row[margin:].reshape(rows, 1)
    seg_row = seg_row.reshape(1, margin + rows)

    got = []
    for first, heads in GROUPS:
        cols = slice(first * HD, (first + heads) * HD)
        pack = jnp.stack([keys[:, cols], values[:, cols]])
        one = moved(pack, 1)
        three = moved(pack, 3)
        cut = heads // 2 * HD
        two = moved(one[:, :, :cut], 1), moved(three[:, :, cut:], -1)
        got.append((one, two, three))

    prev = None
    done = None
    tails = []
    for group, at, heads in CALLS:
        first, size = GROUPS[group]
        one, two, three = got[group]
        half = size // 2
        split = min(max(half - at, 0), heads)
        if 0 < split < heads:
            mid = (jnp.concatenate(two, 2), 0)
        else:
            mid = (two[0], at) if split else (two[1], at - half)
        asked = queries
        if prev is None:
            asked = after(queries, got[1][::2])
        if len(tails) == 3:
            asked = after(queries, [t[4] for t in tails[:2]])
        outs = attend(
            first + at, heads, split, seg_col, seg_row, asked, grad_out, keys, values,
            ((one, at), mid, (three, at)), prev,
        )
        prev, (own, keep, back1, *sent) = outs[:2], outs[2:]
        near = moved(back1, -1)
        if split:
            far = moved(sent[0], -3)
            relay = after((keep[:split] + near[:split]), far)
            tails.append((first + at, split, (own, 0), (far, 0), relay, -1))
        if split < heads:
            ahead = moved(sent[-1], 1)
            relay = after((keep[split:] + ahead), near)
            tails.append((first + at + split, heads - split, (own, split), (near, split), relay, -3))
    for first, heads, own, other, relay, steps in tails:
        done = finish(first, heads, (own, other, (moved(relay, steps), 0)), done)
    return prev[0], prev[1], done[0], done[1]


def solution(mesh):
    spec = P(AXES, None)
    return jax.shard_map(
        shards,
        mesh=mesh,
        in_specs=(spec, spec, spec, spec, P()),
        out_specs=(spec, spec, spec, spec),
        check_vma=False,
    )
```

profile of v0, /device:TPU:46, one launch (start us, length us, event | category | flops | bytes accessed | tf_op | source)
XLA Modules:
  0.0 172.0 jit_solution(11750599856487369971)
XLA Ops:
  0.6 1.3 slice_bitcast_fusion
  1.9 0.8 pad_maximum_fusion.1
  2.7 3.3 %collective-permute-start.2 = (bf16[2,256,512]{2,1,0:T(8,128)(2,1)}, bf16[2,256,512]{2,1,0:T(8,128)(2,1)S(1)}, u32[]{:S(2)}, u32[]{:S(2)}) collective-permute-start(bf16[2,256,512]{2,1,0:T(8,128)(2,1)} %pad_maximum_fusion.1), channel_id=1, source_target_pairs={{0,1},{1,2},{2,3},{3,4},{4,5},{5,6},{6,7},{7,8},{8,9},{9,10},{10,1... | collective-permute-start | bytes 1572872 | tf_op jit(solution)/shard_map/ppermute | solution.py:26
  6.9 3.6 %collective-permute-start = (bf16[2,256,512]{2,1,0:T(8,128)(2,1)}, bf16[2,256,512]{2,1,0:T(8,128)(2,1)S(1)}, u32[]{:S(2)}, u32[]{:S(2)}) collective-permute-start(bf16[2,256,512]{2,1,0:T(8,128)(2,1)} %pad_maximum_fusion), channel_id=1, source_target_pairs={{0,1},{1,2},{2,3},{3,4},{4,5},{5,6},{6,7},{7,8},{8,9},{9,10},{10,1... | collective-permute-start | bytes 1572872 | tf_op jit(solution)/shard_map/ppermute | solution.py:26
  10.4 1.6 collective-permute-start.1
  12.0 0.9 collective-permute-start.4
  12.9 29.7 %collective-permute-done.2.refs_2_.refs_3_ = bf16[2,256,512]{2,1,0:T(8,128)(2,1)S(1)} collective-permute-done((bf16[2,256,512]{2,1,0:T(8,128)(2,1)}, bf16[2,256,512]{2,1,0:T(8,128)(2,1)S(1)}, u32[]{:S(2)}, u32[]{:S(2)}) %collective-permute-start.2) | collective-permute-done | bytes 524320 | tf_op jit(solution)/shard_map/ppermute | solution.py:26
  44.1 1.1 collective-permute-start.3
  46.1 13.9 %collective-permute-done.refs_2_.refs_3_ = bf16[2,256,512]{2,1,0:T(8,128)(2,1)S(1)} collective-permute-done((bf16[2,256,512]{2,1,0:T(8,128)(2,1)}, bf16[2,256,512]{2,1,0:T(8,128)(2,1)S(1)}, u32[]{:S(2)}, u32[]{:S(2)}) %collective-permute-start) | collective-permute-done | bytes 524320 | tf_op jit(solution)/shard_map/ppermute | solution.py:26
  60.0 1.0 slice.37
  61.0 2.4 %collective-permute-start.7 = (bf16[2,256,256]{2,1,0:T(8,128)(2,1)S(1)}, bf16[2,256,256]{2,1,0:T(8,128)(2,1)S(1)}, u32[]{:S(2)}, u32[]{:S(2)}) collective-permute-start(bf16[2,256,256]{2,1,0:T(8,128)(2,1)S(1)} %slice.37), channel_id=1, source_target_pairs={{0,255},{1,0},{2,1},{3,2},{4,3},{5,4},{6,5},{7,6},{8,7},{9,8},{10,... | collective-permute-start | bytes 786440 | tf_op jit(solution)/shard_map/ppermute | solution.py:26
  64.1 4.5 %collective-permute-start.10 = (bf16[2,256,256]{2,1,0:T(8,128)(2,1)S(1)}, bf16[2,256,256]{2,1,0:T(8,128)(2,1)S(1)}, u32[]{:S(2)}, u32[]{:S(2)}) collective-permute-start(bf16[2,256,256]{2,1,0:T(8,128)(2,1)S(1)} %slice.38), channel_id=1, source_target_pairs={{0,255},{1,0},{2,1},{3,2},{4,3},{5,4},{6,5},{7,6},{8,7},{9,8},{10,... | collective-permute-start | bytes 786440 | tf_op jit(solution)/shard_map/ppermute | solution.py:26
  68.6 1.0 copy-done.1
  69.6 1.0 copy-done.2
  70.7 1.0 copy-done.4
  71.7 9.8 %attend.4 = (bf16[256,4096]{1,0:T(8,128)(2,1)}, bf16[256,4096]{1,0:T(8,128)(2,1)}, f32[2,2,256,128]{3,2,1,0:T(8,128)S(1)}, bf16[2,2,256,128]{3,2,1,0:T(8,128)(2,...) custom-call(s32[256,1]{1,0:T(8,128)S(1)} %copy.24.seg_col, s32[1,1024]{1,0:T(1,128)S(1)} %bitcast.10, ...), custom_call_target="tpu_custom_call" | custom-call | flops 3221225472 | bytes 8388608 | tf_op jit(solution)/shard_map/attend/pallas_call | solution.py:146
  82.7 5.7 %collective-permute-start.6 = (bf16[2,2,256,128]{3,2,1,0:T(8,128)(2,1)S(1)}, bf16[2,2,256,128]{3,2,1,0:T(8,128)(2,1)S(1)}, u32[]{:S(2)}, u32[]{:S(2)}) collective-permute-start(bf16[2,2,256,128]{3,2,1,0:T(8,128)(2,1)S(1)} %get-tuple-element.45), channel_id=1, source_target_pairs={{0,253},{1,254},{2,255},{3,0},{4,1},{5,2},{6,3},{7,4},{8,5},{9,6},... | collective-permute-start | bytes 786440 | tf_op jit(solution)/shard_map/ppermute | solution.py:26
  88.4 9.8 %attend.5 = (bf16[256,4096]{1,0:T(8,128)(2,1)}, bf16[256,4096]{1,0:T(8,128)(2,1)}, f32[2,2,256,128]{3,2,1,0:T(8,128)S(1)}, bf16[2,2,256,128]{3,2,1,0:T(8,128)(2,...) custom-call(s32[256,1]{1,0:T(8,128)S(1)} %copy.24.seg_col, ...), custom_call_target="tpu_custom_call", output_to_operand_aliasing={{0}: (12, {}), {1}: (13, {})} | custom-call | flops 3221225472 | bytes 8388608 | tf_op jit(solution)/shard_map/attend/pallas_call | solution.py:146
  99.1 4.9 %collective-permute-start.9 = (bf16[2,2,256,128]{3,2,1,0:T(8,128)(2,1)S(1)}, bf16[2,2,256,128]{3,2,1,0:T(8,128)(2,1)S(1)}, u32[]{:S(2)}, u32[]{:S(2)}) collective-permute-start(bf16[2,2,256,128]{3,2,1,0:T(8,128)(2,1)S(1)} %get-tuple-element.51), channel_id=1, source_target_pairs={{0,255},{1,0},{2,1},{3,2},{4,3},{5,4},{6,5},{7,6},{8,7},{9,8},{10,... | collective-permute-start | bytes 786440 | tf_op jit(solution)/shard_map/ppermute | solution.py:26
  104.0 9.8 %attend.6 = (bf16[256,4096]{1,0:T(8,128)(2,1)}, bf16[256,4096]{1,0:T(8,128)(2,1)}, f32[2,2,256,128]{3,2,1,0:T(8,128)S(1)}, bf16[2,2,256,128]{3,2,1,0:T(8,128)(2,...) custom-call(s32[256,1]{1,0:T(8,128)S(1)} %copy.24.seg_col, ...), custom_call_target="tpu_custom_call", output_to_operand_aliasing={{0}: (12, {}), {1}: (13, {})} | custom-call | flops 3221225472 | bytes 8388608 | tf_op jit(solution)/shard_map/attend/pallas_call | solution.py:146
  114.0 2.3 %collective-permute-start.15 = (bf16[2,2,256,128]{3,2,1,0:T(8,128)(2,1)S(1)}, bf16[2,2,256,128]{3,2,1,0:T(8,128)(2,1)S(1)}, u32[]{:S(2)}, u32[]{:S(2)}) collective-permute-start(bf16[2,2,256,128]{3,2,1,0:T(8,128)(2,1)S(1)} %get-tuple-element.66), channel_id=1, source_target_pairs={{0,253},{1,254},{2,255},{3,0},{4,1},{5,2},{6,3},{7,4},{8,5},{9,6},... | collective-permute-start | bytes 786440 | tf_op jit(solution)/shard_map/ppermute | solution.py:26
  116.4 9.8 %attend.7 = (bf16[256,4096]{1,0:T(8,128)(2,1)}, bf16[256,4096]{1,0:T(8,128)(2,1)}, f32[2,2,256,128]{3,2,1,0:T(8,128)S(1)}, bf16[2,2,256,128]{3,2,1,0:T(8,128)(2,...) custom-call(s32[256,1]{1,0:T(8,128)S(1)} %copy.24.seg_col, ...), custom_call_target="tpu_custom_call", output_to_operand_aliasing={{0}: (12, {}), {1}: (13, {})} | custom-call | flops 3221225472 | bytes 8388608 | tf_op jit(solution)/shard_map/attend/pallas_call | solution.py:146
  127.0 1.0 collective-permute-start.13
  128.0 4.1 %collective-permute-start.12 = (bf16[2,2,256,128]{3,2,1,0:T(8,128)(2,1)S(1)}, bf16[2,2,256,128]{3,2,1,0:T(8,128)(2,1)S(1)}, u32[]{:S(2)}, u32[]{:S(2)}) collective-permute-start(bf16[2,2,256,128]{3,2,1,0:T(8,128)(2,1)S(1)} %get-tuple-element.61), channel_id=1, source_target_pairs={{0,255},{1,0},{2,1},{3,2},{4,3},{5,4},{6,5},{7,6},{8,7},{9,8},{10,... | collective-permute-start | bytes 786440 | tf_op jit(solution)/shard_map/ppermute | solution.py:26
  132.1 3.6 %collective-permute-start.18 = (bf16[2,2,256,128]{3,2,1,0:T(8,128)(2,1)S(1)}, bf16[2,2,256,128]{3,2,1,0:T(8,128)(2,1)S(1)}, u32[]{:S(2)}, u32[]{:S(2)}) collective-permute-start(bf16[2,2,256,128]{3,2,1,0:T(8,128)(2,1)S(1)} %add.23), channel_id=1, source_target_pairs={{0,253},{1,254},{2,255},{3,0},{4,1},{5,2},{6,3},{7,4},{8,5},{9,6},... | collective-permute-start | bytes 786440 | tf_op jit(solution)/shard_map/ppermute | solution.py:26
  135.8 3.7 %collective-permute-start.17 = (bf16[2,2,256,128]{3,2,1,0:T(8,128)(2,1)S(1)}, bf16[2,2,256,128]{3,2,1,0:T(8,128)(2,1)S(1)}, u32[]{:S(2)}, u32[]{:S(2)}) collective-permute-start(bf16[2,2,256,128]{3,2,1,0:T(8,128)(2,1)S(1)} %add.25), channel_id=1, source_target_pairs={{0,255},{1,0},{2,1},{3,2},{4,3},{5,4},{6,5},{7,6},{8,7},{9,8},{10,... | collective-permute-start | bytes 786440 | tf_op jit(solution)/shard_map/ppermute | solution.py:26
  139.5 10.9 %collective-permute-done.13 = bf16[2,2,256,128]{3,2,1,0:T(8,128)(2,1)S(1)} collective-permute-done((bf16[2,2,256,128]{3,2,1,0:T(8,128)(2,1)S(1)}, bf16[2,2,256,128]{3,2,1,0:T(8,128)(2,1)S(1)}, u32[]{:S(2)}, u32[]{:S(2)}) %collective-permute-start.13) | collective-permute-done | bytes 262176 | tf_op jit(solution)/shard_map/ppermute | solution.py:26
  151.3 1.9 %finish.4 = (bf16[256,1024]{1,0:T(8,128)(2,1)}, bf16[256,1024]{1,0:T(8,128)(2,1)}) custom-call(f32[2,2,256,128]{3,2,1,0:T(8,128)} %copy-done.5, bf16[2,2,256,128]{3,2,1,0:T(8,128)(2,1)} %copy-done.9, bf16[2,2,256,128]{3,2,1,0:T(8,128)(2,1)} %copy-done.10), custom_call_target="tpu_custom_call" | custom-call | flops 1000000 | bytes 3145728 | tf_op jit(solution)/shard_map/finish/pallas_call | solution.py:193
  153.9 1.9 %finish.5 = (bf16[256,1024]{1,0:T(8,128)(2,1)}, bf16[256,1024]{1,0:T(8,128)(2,1)}) custom-call(f32[2,2,256,128]{3,2,1,0:T(8,128)} %copy-done.6, bf16[2,2,256,128]{3,2,1,0:T(8,128)(2,1)} %copy-done.11, bf16[2,2,256,128]{3,2,1,0:T(8,128)(2,1)} %copy-done.16, ...), custom_call_target="tpu_custom_call", output_to_operand_aliasing={{0}: (3, {}), {1}: (4, {})} | custom-call | flops 1000000 | bytes 3145728 | tf_op jit(solution)/shard_map/finish/pallas_call | solution.py:193
  155.9 10.8 %collective-permute-done.17.b = bf16[2,2,256,128]{3,2,1,0:T(8,128)(2,1)S(1)} collective-permute-done((bf16[2,2,256,128]{3,2,1,0:T(8,128)(2,1)S(1)}, bf16[2,2,256,128]{3,2,1,0:T(8,128)(2,1)S(1)}, u32[]{:S(2)}, u32[]{:S(2)}) %collective-permute-start.17) | collective-permute-done | bytes 262176 | tf_op jit(solution)/shard_map/ppermute | solution.py:26
  167.4 1.9 %finish.6 = (bf16[256,1024]{1,0:T(8,128)(2,1)}, bf16[256,1024]{1,0:T(8,128)(2,1)}) custom-call(f32[2,2,256,128]{3,2,1,0:T(8,128)} %copy-done.7, bf16[2,2,256,128]{3,2,1,0:T(8,128)(2,1)} %copy-done.12, bf16[2,2,256,128]{3,2,1,0:T(8,128)(2,1)} %copy-done.14, ...), custom_call_target="tpu_custom_call", output_to_operand_aliasing={{0}: (3, {}), {1}: (4, {})} | custom-call | flops 1000000 | bytes 3145728 | tf_op jit(solution)/shard_map/finish/pallas_call | solution.py:193
  170.0 1.9 %finish.7 = (bf16[256,1024]{1,0:T(8,128)(2,1)}, bf16[256,1024]{1,0:T(8,128)(2,1)}) custom-call(f32[2,2,256,128]{3,2,1,0:T(8,128)} %copy-done.8, bf16[2,2,256,128]{3,2,1,0:T(8,128)(2,1)} %copy-done.13, bf16[2,2,256,128]{3,2,1,0:T(8,128)(2,1)} %copy-done.15, ...), custom_call_target="tpu_custom_call", output_to_operand_aliasing={{0}: (3, {}), {1}: (4, {})} | custom-call | flops 1000000 | bytes 3145728 | tf_op jit(solution)/shard_map/finish/pallas_call | solution.py:193
  (64 shorter events, 10.3 us)
Async XLA Ops:
  1.9 66.7 %copy-start = (bf16[256,4096]{1,0:T(8,128)(2,1)S(1)}, bf16[256,4096]{1,0:T(8,128)(2,1)}, u32[]{:S(2)}) copy-start(bf16[256,4096]{1,0:T(8,128)(2,1)} %q.5) | copy-start | bytes 6291460
  2.7 39.8 %collective-permute-start.2 = (bf16[2,256,512]{2,1,0:T(8,128)(2,1)}, bf16[2,256,512]{2,1,0:T(8,128)(2,1)S(1)}, u32[]{:S(2)}, u32[]{:S(2)}) collective-permute-start(bf16[2,256,512]{2,1,0:T(8,128)(2,1)} %pad_maximum_fusion.1), channel_id=1, source_target_pairs={{0,1},{1,2},{2,3},{3,4},{4,5},{5,6},{6,7},{7,8},{8,9},{9,10},{10,1... | collective-permute-start | bytes 1572872 | tf_op jit(solution)/shard_map/ppermute | solution.py:26
  6.9 53.1 %collective-permute-start = (bf16[2,256,512]{2,1,0:T(8,128)(2,1)}, bf16[2,256,512]{2,1,0:T(8,128)(2,1)S(1)}, u32[]{:S(2)}, u32[]{:S(2)}) collective-permute-start(bf16[2,256,512]{2,1,0:T(8,128)(2,1)} %pad_maximum_fusion), channel_id=1, source_target_pairs={{0,1},{1,2},{2,3},{3,4},{4,5},{5,6},{6,7},{7,8},{8,9},{9,10},{10,1... | collective-permute-start | bytes 1572872 | tf_op jit(solution)/shard_map/ppermute | solution.py:26
  10.4 49.6 %collective-permute-start.1 = (bf16[2,256,512]{2,1,0:T(8,128)(2,1)}, bf16[2,256,512]{2,1,0:T(8,128)(2,1)S(1)}, u32[]{:S(2)}, u32[]{:S(2)}) collective-permute-start(bf16[2,256,512]{2,1,0:T(8,128)(2,1)} %pad_maximum_fusion), channel_id=1, source_target_pairs={{0,3},{1,4},{2,5},{3,6},{4,7},{5,8},{6,9},{7,10},{8,11},{9,12},{10... | collective-permute-start | bytes 1572872 | tf_op jit(solution)/shard_map/ppermute | solution.py:26
  12.0 48.0 %collective-permute-start.4 = (bf16[2,256,512]{2,1,0:T(8,128)(2,1)}, bf16[2,256,512]{2,1,0:T(8,128)(2,1)}, u32[]{:S(2)}, u32[]{:S(2)}) collective-permute-start(bf16[2,256,512]{2,1,0:T(8,128)(2,1)} %pad_maximum_fusion.1), channel_id=1, source_target_pairs={{0,3},{1,4},{2,5},{3,6},{4,7},{5,8},{6,9},{7,10},{8,11},{9,12},{10... | collective-permute-start | bytes 1572872 | tf_op jit(solution)/shard_map/ppermute | solution.py:26
  43.3 0.8 copy-start.3
  44.1 24.5 %collective-permute-start.3 = (bf16[2,256,256]{2,1,0:T(8,128)(2,1)}, bf16[2,256,256]{2,1,0:T(8,128)(2,1)S(1)}, u32[]{:S(2)}, u32[]{:S(2)}) collective-permute-start(bf16[2,256,256]{2,1,0:T(8,128)(2,1)} %slice.36), channel_id=1, source_target_pairs={{0,1},{1,2},{2,3},{3,4},{4,5},{5,6},{6,7},{7,8},{8,9},{9,10},{10,1... | collective-permute-start | bytes 786440 | tf_op jit(solution)/shard_map/ppermute | solution.py:26
  61.0 27.4 %collective-permute-start.7 = (bf16[2,256,256]{2,1,0:T(8,128)(2,1)S(1)}, bf16[2,256,256]{2,1,0:T(8,128)(2,1)S(1)}, u32[]{:S(2)}, u32[]{:S(2)}) collective-permute-start(bf16[2,256,256]{2,1,0:T(8,128)(2,1)S(1)} %slice.37), channel_id=1, source_target_pairs={{0,255},{1,0},{2,1},{3,2},{4,3},{5,4},{6,5},{7,6},{8,7},{9,8},{10,... | collective-permute-start | bytes 786440 | tf_op jit(solution)/shard_map/ppermute | solution.py:26
  63.4 35.7 %collective-permute-start.11 = (bf16[2,256,256]{2,1,0:T(8,128)(2,1)S(1)}, bf16[2,256,256]{2,1,0:T(8,128)(2,1)S(1)}, u32[]{:S(2)}, u32[]{:S(2)}) collective-permute-start(bf16[2,256,256]{2,1,0:T(8,128)(2,1)S(1)} %slice.39), channel_id=1, source_target_pairs={{0,1},{1,2},{2,3},{3,4},{4,5},{5,6},{6,7},{7,8},{8,9},{9,10},{10,1... | collective-permute-start | bytes 786440 | tf_op jit(solution)/shard_map/ppermute | solution.py:26
  64.1 52.2 %collective-permute-start.10 = (bf16[2,256,256]{2,1,0:T(8,128)(2,1)S(1)}, bf16[2,256,256]{2,1,0:T(8,128)(2,1)S(1)}, u32[]{:S(2)}, u32[]{:S(2)}) collective-permute-start(bf16[2,256,256]{2,1,0:T(8,128)(2,1)S(1)} %slice.38), channel_id=1, source_target_pairs={{0,255},{1,0},{2,1},{3,2},{4,3},{5,4},{6,5},{7,6},{8,7},{9,8},{10,... | collective-permute-start | bytes 786440 | tf_op jit(solution)/shard_map/ppermute | solution.py:26
  68.6 1.0 copy-start.1
  69.6 1.0 copy-start.2
  70.7 1.0 copy-start.4
  81.5 0.8 copy-start.5
  82.3 31.5 %collective-permute-start.5 = (bf16[2,2,256,128]{3,2,1,0:T(8,128)(2,1)S(1)}, bf16[2,2,256,128]{3,2,1,0:T(8,128)(2,1)S(1)}, u32[]{:S(2)}, u32[]{:S(2)}) collective-permute-start(bf16[2,2,256,128]{3,2,1,0:T(8,128)(2,1)S(1)} %get-tuple-element.44), channel_id=1, source_target_pairs={{0,255},{1,0},{2,1},{3,2},{4,3},{5,4},{6,5},{7,6},{8,7},{9,8},{10,... | collective-permute-start | bytes 786440 | tf_op jit(solution)/shard_map/ppermute | solution.py:26
  82.7 31.3 %collective-permute-start.6 = (bf16[2,2,256,128]{3,2,1,0:T(8,128)(2,1)S(1)}, bf16[2,2,256,128]{3,2,1,0:T(8,128)(2,1)S(1)}, u32[]{:S(2)}, u32[]{:S(2)}) collective-permute-start(bf16[2,2,256,128]{3,2,1,0:T(8,128)(2,1)S(1)} %get-tuple-element.45), channel_id=1, source_target_pairs={{0,253},{1,254},{2,255},{3,0},{4,1},{5,2},{6,3},{7,4},{8,5},{9,6},... | collective-permute-start | bytes 786440 | tf_op jit(solution)/shard_map/ppermute | solution.py:26
  98.2 0.8 copy-start.6
  99.0 17.3 %collective-permute-start.8 = (bf16[2,2,256,128]{3,2,1,0:T(8,128)(2,1)S(1)}, bf16[2,2,256,128]{3,2,1,0:T(8,128)(2,1)S(1)}, u32[]{:S(2)}, u32[]{:S(2)}) collective-permute-start(bf16[2,2,256,128]{3,2,1,0:T(8,128)(2,1)S(1)} %get-tuple-element.50), channel_id=1, source_target_pairs={{0,1},{1,2},{2,3},{3,4},{4,5},{5,6},{6,7},{7,8},{8,9},{9,10},{10,1... | collective-permute-start | bytes 786440 | tf_op jit(solution)/shard_map/ppermute | solution.py:26
  99.1 17.2 %collective-permute-start.9 = (bf16[2,2,256,128]{3,2,1,0:T(8,128)(2,1)S(1)}, bf16[2,2,256,128]{3,2,1,0:T(8,128)(2,1)S(1)}, u32[]{:S(2)}, u32[]{:S(2)}) collective-permute-start(bf16[2,2,256,128]{3,2,1,0:T(8,128)(2,1)S(1)} %get-tuple-element.51), channel_id=1, source_target_pairs={{0,255},{1,0},{2,1},{3,2},{4,3},{5,4},{6,5},{7,6},{8,7},{9,8},{10,... | collective-permute-start | bytes 786440 | tf_op jit(solution)/shard_map/ppermute | solution.py:26
  113.8 12.4 %copy-start.7 = (f32[2,2,256,128]{3,2,1,0:T(8,128)}, f32[2,2,256,128]{3,2,1,0:T(8,128)S(1)}, u32[]{:S(2)}) copy-start(f32[2,2,256,128]{3,2,1,0:T(8,128)S(1)} %get-tuple-element.65.own) | copy-start | bytes 1572868
  113.8 18.3 %collective-permute-start.16 = (bf16[2,2,256,128]{3,2,1,0:T(8,128)(2,1)S(1)}, bf16[2,2,256,128]{3,2,1,0:T(8,128)(2,1)S(1)}, u32[]{:S(2)}, u32[]{:S(2)}) collective-permute-start(bf16[2,2,256,128]{3,2,1,0:T(8,128)(2,1)S(1)} %get-tuple-element.68), channel_id=1, source_target_pairs={{0,255},{1,0},{2,1},{3,2},{4,3},{5,4},{6,5},{7,6},{8,7},{9,8},{10,... | collective-permute-start | bytes 786440 | tf_op jit(solution)/shard_map/ppermute | solution.py:26
  114.0 12.2 %copy-start.9 = (bf16[2,2,256,128]{3,2,1,0:T(8,128)(2,1)}, bf16[2,2,256,128]{3,2,1,0:T(8,128)(2,1)S(1)}, u32[]{:S(2)}) copy-start(bf16[2,2,256,128]{3,2,1,0:T(8,128)(2,1)S(1)} %collective-permute-done.6.a) | copy-start | bytes 786436
  114.0 21.8 %collective-permute-start.15 = (bf16[2,2,256,128]{3,2,1,0:T(8,128)(2,1)S(1)}, bf16[2,2,256,128]{3,2,1,0:T(8,128)(2,1)S(1)}, u32[]{:S(2)}, u32[]{:S(2)}) collective-permute-start(bf16[2,2,256,128]{3,2,1,0:T(8,128)(2,1)S(1)} %get-tuple-element.66), channel_id=1, source_target_pairs={{0,253},{1,254},{2,255},{3,0},{4,1},{5,2},{6,3},{7,4},{8,5},{9,6},... | collective-permute-start | bytes 786440 | tf_op jit(solution)/shard_map/ppermute | solution.py:26
  116.3 9.9 %copy-start.11 = (bf16[2,2,256,128]{3,2,1,0:T(8,128)(2,1)}, bf16[2,2,256,128]{3,2,1,0:T(8,128)(2,1)S(1)}, u32[]{:S(2)}) copy-start(bf16[2,2,256,128]{3,2,1,0:T(8,128)(2,1)S(1)} %collective-permute-done.9.a) | copy-start | bytes 786436
  127.0 23.4 %collective-permute-start.13 = (bf16[2,2,256,128]{3,2,1,0:T(8,128)(2,1)S(1)}, bf16[2,2,256,128]{3,2,1,0:T(8,128)(2,1)S(1)}, u32[]{:S(2)}, u32[]{:S(2)}) collective-permute-start(bf16[2,2,256,128]{3,2,1,0:T(8,128)(2,1)S(1)} %get-tuple-element.63), channel_id=1, source_target_pairs={{0,1},{1,2},{2,3},{3,4},{4,5},{5,6},{6,7},{7,8},{8,9},{9,10},{10,1... | collective-permute-start | bytes 786440 | tf_op jit(solution)/shard_map/ppermute | solution.py:26
  128.0 22.5 %collective-permute-start.12 = (bf16[2,2,256,128]{3,2,1,0:T(8,128)(2,1)S(1)}, bf16[2,2,256,128]{3,2,1,0:T(8,128)(2,1)S(1)}, u32[]{:S(2)}, u32[]{:S(2)}) collective-permute-start(bf16[2,2,256,128]{3,2,1,0:T(8,128)(2,1)S(1)} %get-tuple-element.61), channel_id=1, source_target_pairs={{0,255},{1,0},{2,1},{3,2},{4,3},{5,4},{6,5},{7,6},{8,7},{9,8},{10,... | collective-permute-start | bytes 786440 | tf_op jit(solution)/shard_map/ppermute | solution.py:26
  132.0 18.5 %collective-permute-start.19 = (bf16[2,2,256,128]{3,2,1,0:T(8,128)(2,1)S(1)}, bf16[2,2,256,128]{3,2,1,0:T(8,128)(2,1)S(1)}, u32[]{:S(2)}, u32[]{:S(2)}) collective-permute-start(bf16[2,2,256,128]{3,2,1,0:T(8,128)(2,1)S(1)} %add.22), channel_id=1, source_target_pairs={{0,255},{1,0},{2,1},{3,2},{4,3},{5,4},{6,5},{7,6},{8,7},{9,8},{10,... | collective-permute-start | bytes 786440 | tf_op jit(solution)/shard_map/ppermute | solution.py:26
  132.1 21.2 %collective-permute-start.18 = (bf16[2,2,256,128]{3,2,1,0:T(8,128)(2,1)S(1)}, bf16[2,2,256,128]{3,2,1,0:T(8,128)(2,1)S(1)}, u32[]{:S(2)}, u32[]{:S(2)}) collective-permute-start(bf16[2,2,256,128]{3,2,1,0:T(8,128)(2,1)S(1)} %add.23), channel_id=1, source_target_pairs={{0,253},{1,254},{2,255},{3,0},{4,1},{5,2},{6,3},{7,4},{8,5},{9,6},... | collective-permute-start | bytes 786440 | tf_op jit(solution)/shard_map/ppermute | solution.py:26
  135.8 14.8 %copy-start.12 = (bf16[2,2,256,128]{3,2,1,0:T(8,128)(2,1)}, bf16[2,2,256,128]{3,2,1,0:T(8,128)(2,1)S(1)}, u32[]{:S(2)}) copy-start(bf16[2,2,256,128]{3,2,1,0:T(8,128)(2,1)S(1)} %collective-permute-done.15.a) | copy-start | bytes 786436
  135.8 30.9 %collective-permute-start.17 = (bf16[2,2,256,128]{3,2,1,0:T(8,128)(2,1)S(1)}, bf16[2,2,256,128]{3,2,1,0:T(8,128)(2,1)S(1)}, u32[]{:S(2)}, u32[]{:S(2)}) collective-permute-start(bf16[2,2,256,128]{3,2,1,0:T(8,128)(2,1)S(1)} %add.25), channel_id=1, source_target_pairs={{0,255},{1,0},{2,1},{3,2},{4,3},{5,4},{6,5},{7,6},{8,7},{9,8},{10,... | collective-permute-start | bytes 786440 | tf_op jit(solution)/shard_map/ppermute | solution.py:26
  150.5 18.9 %copy-start.13 = (bf16[2,2,256,128]{3,2,1,0:T(8,128)(2,1)}, bf16[2,2,256,128]{3,2,1,0:T(8,128)(2,1)S(1)}, u32[]{:S(2)}) copy-start(bf16[2,2,256,128]{3,2,1,0:T(8,128)(2,1)S(1)} %collective-permute-done.12.a) | copy-start | bytes 786436
  150.5 18.8 %collective-permute-start.14 = (bf16[2,2,256,128]{3,2,1,0:T(8,128)(2,1)S(1)}, bf16[2,2,256,128]{3,2,1,0:T(8,128)(2,1)S(1)}, u32[]{:S(2)}, u32[]{:S(2)}) collective-permute-start(bf16[2,2,256,128]{3,2,1,0:T(8,128)(2,1)S(1)} %add.24), channel_id=1, source_target_pairs={{0,253},{1,254},{2,255},{3,0},{4,1},{5,2},{6,3},{7,4},{8,5},{9,6},... | collective-permute-start | bytes 786440 | tf_op jit(solution)/shard_map/ppermute | solution.py:26
  (5 other events, 3.6 us)
where the time goes:
time: 175 us; the launch traced here: 172 us
  waiting for transfers between devices  65.3 us (37%)
  Pallas kernels  46.9 us (27%)
  starting transfers between devices  43.9 us (25%)
  local copies, waits for them, and re-layouts  13.1 us (7%)
  other arithmetic  1.97 us (1%)
    ppermute x20, waiting for transfers between devices, moved(): lax.ppermute(value, AXES, [(i, (i + steps) % count) for i in range(count)])  65.3 us
    ppermute x20, starting transfers between devices, moved(): lax.ppermute(value, AXES, [(i, (i + steps) % count) for i in range(count)])  43.9 us
    pallas_call x4, Pallas kernels, attend(): pl.pallas_call(functools.partial(attend_kernel, split, heads), grid=(head...  39.2 us
    unnamed x34, local copies, waits for them, and re-layouts  9.15 us
    pallas_call x4, Pallas kernels, finish(): pl.pallas_call(finish_kernel, grid=(heads // unit,), in_specs=specs, out_...  7.72 us
  transfers between devices with their start and end apart: 20, of which 4 were waited for; matrix products, arithmetic and copies ran while one was open for 2% of the time, Pallas kernels for 26%

commit v1 on v0

--- a/solution.py
+++ b/solution.py
@@ -81,7 +81,7 @@
         dog = (do[:, cols].astype(jnp.float32) * inv).astype(jnp.bfloat16)
         delta = jnp.sum(dog.astype(jnp.float32) * out.astype(jnp.float32), axis=1, keepdims=True)
         dp = dot_nt(dog, vcat[...])
-        ds[g % 2] = (ph[g % 2].astype(jnp.float32) * (dp - delta)).astype(jnp.bfloat16)
+        ds[g % 2] = ph[g % 2] * (dp - delta).astype(jnp.bfloat16)
         if g + 1 < GROUP:
             inv = exponent(g + 1)
         dq[:, cols] = (dot_nn(ds[g % 2], kcat[...]) * scale).astype(jnp.bfloat16)
@@ -162,43 +162,11 @@
             pltpu.VMEM((2, rows, BLOCKS * rows), jnp.bfloat16),
         ],
         input_output_aliases=aliases,
-        compiler_params=pltpu.CompilerParams(vmem_limit_bytes=48 * 1024 * 1024),
+        compiler_params=pltpu.CompilerParams(vmem_limit_bytes=60 * 1024 * 1024),
         cost_estimate=pl.CostEstimate(
             flops=flops, bytes_accessed=8 * 2**20, transcendentals=rows * rows * 4 * GROUP * heads
         ),
         name="attend",
-    )(*args)
-
-
-def finish_kernel(own, a, b, *refs):
-    for part, ref in enumerate(refs[-2:]):
-        for h in range(own.shape[0]):
-            total = own[h, part] + a[h, part].astype(jnp.float32) + b[h, part].astype(jnp.float32)
-            ref[:, h * HD : (h + 1) * HD] = total.astype(jnp.bfloat16)
-
-
-def finish(first, heads, terms, prev):
-    rows = terms[0][0].shape[2]
-    unit = 2 if all(x % 2 == 0 for x in (first, heads, *[at for _, at in terms])) else 1
-    specs = [
-        pl.BlockSpec((unit, 2, rows, HD), lambda i, at=at: (at // unit + i, 0, 0, 0))
-        for _, at in terms
-    ]
-    args, aliases = [t for t, _ in terms], {}
-    out = pl.BlockSpec((rows, unit * HD), lambda i: (0, first // unit + i))
-    if prev is not None:
-        aliases = {3: 0, 4: 1}
-        specs = specs + [pl.BlockSpec(memory_space=pl.ANY)] * 2
-        args += list(prev)
-    return pl.pallas_call(
-        finish_kernel,
-        grid=(heads // unit,),
-        in_specs=specs,
-        out_specs=[out, out],
-        out_shape=[jax.ShapeDtypeStruct((rows, HK * HD), jnp.bfloat16)] * 2,
-        input_output_aliases=aliases,
-        cost_estimate=pl.CostEstimate(flops=10**6, bytes_accessed=3 * 2**20, transcendentals=0),
-        name="finish",
     )(*args)
 
 
@@ -252,9 +220,21 @@
             ahead = moved(sent[-1], 1)
             relay = after((keep[split:] + ahead), near)
             tails.append((first + at + split, heads - split, (own, split), (near, split), relay, -3))
-    for first, heads, own, other, relay, steps in tails:
-        done = finish(first, heads, (own, other, (moved(relay, steps), 0)), done)
-    return prev[0], prev[1], done[0], done[1]
+    back = []
+    for *_, relay, steps in tails:
+        back.append(moved(relay, steps))
+    sums = [
+        (own[0] + other[0].astype(jnp.float32) + last.astype(jnp.float32)).astype(jnp.bfloat16)
+        for (_, _, own, other, _, _), last in zip(tails, back)
+    ]
+    grads = []
+    for part in range(2):
+        wide = [jnp.concatenate([x[h, part] for h in range(x.shape[0])], 1) for x in sums]
+        early = jnp.concatenate([*wide[:-1], jnp.zeros_like(wide[-1])], 1)
+        early = lax.optimization_barrier(early)
+        start = early.shape[1] - wide[-1].shape[1]
+        grads.append(lax.dynamic_update_slice(early, wide[-1], (0, start)))
+    return prev[0], prev[1], grads[0], grads[1]
 
 
 def solution(mesh):

time: 175 us -> 169 us (0.966); the launches traced: 172 us -> 169 us
  local copies, waits for them, and re-layouts: 13.1 us -> 5.69 us
  waiting for transfers between devices: 65.3 us -> 72.7 us
  Pallas kernels: 46.9 us -> 40.3 us
  starting transfers between devices: 43.9 us -> 48.4 us
    pallas_call x4 -> x0, Pallas kernels: 7.72 us -> none  [finish(): pl.pallas_call(finish_kernel, grid=(heads // unit,), in_specs=specs, out_...]
    ppermute x20, waiting for transfers between devices: 65.3 us -> 72.7 us  [moved(): lax.ppermute(value, AXES, [(i, (i + steps) % count) for i in range(count)])]
    unnamed x34 -> x44, local copies, waits for them, and re-layouts: 9.15 us -> 2.62 us
    ppermute x20, starting transfers between devices: 43.9 us -> 48.4 us  [moved(): lax.ppermute(value, AXES, [(i, (i + steps) % count) for i in range(count)])]
  transfers between devices with their start and end apart: 20 -> 20, of which waited for: 4 -> 8; matrix products, arithmetic and copies ran while one was open for 2% -> 2% of each run, Pallas kernels for 26% -> 24%
where the time goes in v1:
time: 169 us
  waiting for transfers between devices  72.7 us (43%)
  starting transfers between devices  48.4 us (29%)
  Pallas kernels  40.3 us (24%)
  local copies, waits for them, and re-layouts  5.69 us (3%)
    ppermute x20, waiting for transfers between devices, moved(): lax.ppermute(value, AXES, [(i, (i + steps) % count) for i in range(count)])  72.7 us
    ppermute x20, starting transfers between devices, moved(): lax.ppermute(value, AXES, [(i, (i + steps) % count) for i in range(count)])  48.4 us
    pallas_call x4, Pallas kernels, attend(): pl.pallas_call(functools.partial(attend_kernel, split, heads), grid=(head...  40.3 us
  transfers between devices with their start and end apart: 20, of which 8 were waited for; matrix products, arithmetic and copies ran while one was open for 2% of the time, Pallas kernels for 24%

profile of v1, /device:TPU:46, one launch (start us, length us, event | category | flops | bytes accessed | tf_op | source)
XLA Modules:
  0.0 168.9 jit_solution(14828287219748211547)
XLA Ops:
  0.6 1.3 slice_bitcast_fusion
  2.0 3.3 %collective-permute-start.2 = (bf16[2,256,512]{2,1,0:T(8,128)(2,1)S(1)}, bf16[2,256,512]{2,1,0:T(8,128)(2,1)S(1)}, u32[]{:S(2)}, u32[]{:S(2)}) collective-permute-start(bf16[2,256,512]{2,1,0:T(8,128)(2,1)S(1)} %pad_maximum_fusion.1), channel_id=1, source_target_pairs={{0,1},{1,2},{2,3},{3,4},{4,5},{5,6},{6,7},{7,8},{8,9},{9,10},{10,1... | collective-permute-start | bytes 1572872 | tf_op jit(solution)/shard_map/ppermute | solution.py:26
  5.4 2.2 %collective-permute-start.1 = (bf16[2,256,512]{2,1,0:T(8,128)(2,1)S(1)}, bf16[2,256,512]{2,1,0:T(8,128)(2,1)S(1)}, u32[]{:S(2)}, u32[]{:S(2)}) collective-permute-start(bf16[2,256,512]{2,1,0:T(8,128)(2,1)S(1)} %pad_maximum_fusion), channel_id=1, source_target_pairs={{0,3},{1,4},{2,5},{3,6},{4,7},{5,8},{6,9},{7,10},{8,11},{9,12},{10... | collective-permute-start | bytes 1572872 | tf_op jit(solution)/shard_map/ppermute | solution.py:26
  7.6 1.8 %collective-permute-start = (bf16[2,256,512]{2,1,0:T(8,128)(2,1)S(1)}, bf16[2,256,512]{2,1,0:T(8,128)(2,1)S(1)}, u32[]{:S(2)}, u32[]{:S(2)}) collective-permute-start(bf16[2,256,512]{2,1,0:T(8,128)(2,1)S(1)} %pad_maximum_fusion), channel_id=1, source_target_pairs={{0,1},{1,2},{2,3},{3,4},{4,5},{5,6},{6,7},{7,8},{8,9},{9,10},{10,1... | collective-permute-start | bytes 1572872 | tf_op jit(solution)/shard_map/ppermute | solution.py:26
  9.4 3.4 %collective-permute-start.4 = (bf16[2,256,512]{2,1,0:T(8,128)(2,1)S(1)}, bf16[2,256,512]{2,1,0:T(8,128)(2,1)S(1)}, u32[]{:S(2)}, u32[]{:S(2)}) collective-permute-start(bf16[2,256,512]{2,1,0:T(8,128)(2,1)S(1)} %pad_maximum_fusion.1), channel_id=1, source_target_pairs={{0,3},{1,4},{2,5},{3,6},{4,7},{5,8},{6,9},{7,10},{8,11},{9,12},{10... | collective-permute-start | bytes 1572872 | tf_op jit(solution)/shard_map/ppermute | solution.py:26
  12.8 34.0 %collective-permute-done.2.refs_2_.refs_3_ = bf16[2,256,512]{2,1,0:T(8,128)(2,1)S(1)} collective-permute-done((bf16[2,256,512]{2,1,0:T(8,128)(2,1)S(1)}, bf16[2,256,512]{2,1,0:T(8,128)(2,1)S(1)}, u32[]{:S(2)}, u32[]{:S(2)}) %collective-permute-start.2) | collective-permute-done | bytes 524320 | tf_op jit(solution)/shard_map/ppermute | solution.py:26
  46.8 0.8 slice.100
  47.5 0.9 collective-permute-start.3
  48.5 0.8 copy.18.seg_col
  49.4 4.2 %collective-permute-start.10 = (bf16[2,256,256]{2,1,0:T(8,128)(2,1)S(1)}, bf16[2,256,256]{2,1,0:T(8,128)(2,1)S(1)}, u32[]{:S(2)}, u32[]{:S(2)}) collective-permute-start(bf16[2,256,256]{2,1,0:T(8,128)(2,1)S(1)} %slice.102), channel_id=1, source_target_pairs={{0,255},{1,0},{2,1},{3,2},{4,3},{5,4},{6,5},{7,6},{8,7},{9,8},{10,... | collective-permute-start | bytes 786440 | tf_op jit(solution)/shard_map/ppermute | solution.py:26
  53.6 5.7 %collective-permute-done.refs_2_.refs_3_ = bf16[2,256,512]{2,1,0:T(8,128)(2,1)S(1)} collective-permute-done((bf16[2,256,512]{2,1,0:T(8,128)(2,1)S(1)}, bf16[2,256,512]{2,1,0:T(8,128)(2,1)S(1)}, u32[]{:S(2)}, u32[]{:S(2)}) %collective-permute-start) | collective-permute-done | bytes 524320 | tf_op jit(solution)/shard_map/ppermute | solution.py:26
  59.5 5.1 %collective-permute-start.7 = (bf16[2,256,256]{2,1,0:T(8,128)(2,1)S(1)}, bf16[2,256,256]{2,1,0:T(8,128)(2,1)S(1)}, u32[]{:S(2)}, u32[]{:S(2)}) collective-permute-start(bf16[2,256,256]{2,1,0:T(8,128)(2,1)S(1)} %slice.101), channel_id=1, source_target_pairs={{0,255},{1,0},{2,1},{3,2},{4,3},{5,4},{6,5},{7,6},{8,7},{9,8},{10,... | collective-permute-start | bytes 786440 | tf_op jit(solution)/shard_map/ppermute | solution.py:26
  64.8 10.1 %attend.4 = (bf16[256,4096]{1,0:T(8,128)(2,1)}, bf16[256,4096]{1,0:T(8,128)(2,1)}, f32[2,2,256,128]{3,2,1,0:T(8,128)}, bf16[2,2,256,128]{3,2,1,0:T(8,128)(2,1)},...) custom-call(s32[256,1]{1,0:T(8,128)} %copy.18.seg_col, s32[1,1024]{1,0:T(1,128)} %bitcast.66, ...), custom_call_target="tpu_custom_call" | custom-call | flops 3221225472 | bytes 8388608 | tf_op jit(solution)/shard_map/attend/pallas_call | solution.py:146
  74.9 2.5 %collective-permute-start.5 = (bf16[2,2,256,128]{3,2,1,0:T(8,128)(2,1)}, bf16[2,2,256,128]{3,2,1,0:T(8,128)(2,1)S(1)}, u32[]{:S(2)}, u32[]{:S(2)}) collective-permute-start(bf16[2,2,256,128]{3,2,1,0:T(8,128)(2,1)} %get-tuple-element.36), channel_id=1, source_target_pairs={{0,255},{1,0},{2,1},{3,2},{4,3},{5,4},{6,5},{7,6},{8,7},{9,8},{10,... | collective-permute-start | bytes 786440 | tf_op jit(solution)/shard_map/ppermute | solution.py:26
  77.5 3.7 %collective-permute-start.6 = (bf16[2,2,256,128]{3,2,1,0:T(8,128)(2,1)}, bf16[2,2,256,128]{3,2,1,0:T(8,128)(2,1)S(1)}, u32[]{:S(2)}, u32[]{:S(2)}) collective-permute-start(bf16[2,2,256,128]{3,2,1,0:T(8,128)(2,1)} %get-tuple-element.37), channel_id=1, source_target_pairs={{0,253},{1,254},{2,255},{3,0},{4,1},{5,2},{6,3},{7,4},{8,5},{9,6},... | collective-permute-start | bytes 786440 | tf_op jit(solution)/shard_map/ppermute | solution.py:26
  81.2 0.7 copy-done.6
  81.9 10.0 %attend.5 = (bf16[256,4096]{1,0:T(8,128)(2,1)}, bf16[256,4096]{1,0:T(8,128)(2,1)}, f32[2,2,256,128]{3,2,1,0:T(8,128)}, bf16[2,2,256,128]{3,2,1,0:T(8,128)(2,1)},...) custom-call(s32[256,1]{1,0:T(8,128)} %copy.18.seg_col, ...), custom_call_target="tpu_custom_call", output_to_operand_aliasing={{0}: (12, {}), {1}: (13, {})} | custom-call | flops 3221225472 | bytes 8388608 | tf_op jit(solution)/shard_map/attend/pallas_call | solution.py:146
  92.2 6.9 %collective-permute-start.9 = (bf16[2,2,256,128]{3,2,1,0:T(8,128)(2,1)}, bf16[2,2,256,128]{3,2,1,0:T(8,128)(2,1)S(1)}, u32[]{:S(2)}, u32[]{:S(2)}) collective-permute-start(bf16[2,2,256,128]{3,2,1,0:T(8,128)(2,1)} %get-tuple-element.43), channel_id=1, source_target_pairs={{0,255},{1,0},{2,1},{3,2},{4,3},{5,4},{6,5},{7,6},{8,7},{9,8},{10,... | collective-permute-start | bytes 786440 | tf_op jit(solution)/shard_map/ppermute | solution.py:26
  99.1 10.1 %attend.6 = (bf16[256,4096]{1,0:T(8,128)(2,1)}, bf16[256,4096]{1,0:T(8,128)(2,1)}, f32[2,2,256,128]{3,2,1,0:T(8,128)}, bf16[2,2,256,128]{3,2,1,0:T(8,128)(2,1)},...) custom-call(s32[256,1]{1,0:T(8,128)} %copy.18.seg_col, ...), custom_call_target="tpu_custom_call", output_to_operand_aliasing={{0}: (12, {}), {1}: (13, {})} | custom-call | flops 3221225472 | bytes 8388608 | tf_op jit(solution)/shard_map/attend/pallas_call | solution.py:146
  109.4 2.9 %collective-permute-start.15 = (bf16[2,2,256,128]{3,2,1,0:T(8,128)(2,1)}, bf16[2,2,256,128]{3,2,1,0:T(8,128)(2,1)S(1)}, u32[]{:S(2)}, u32[]{:S(2)}) collective-permute-start(bf16[2,2,256,128]{3,2,1,0:T(8,128)(2,1)} %get-tuple-element.57), channel_id=1, source_target_pairs={{0,255},{1,0},{2,1},{3,2},{4,3},{5,4},{6,5},{7,6},{8,7},{9,8},{10,... | collective-permute-start | bytes 786440 | tf_op jit(solution)/shard_map/ppermute | solution.py:26
  112.3 0.7 collective-permute-start.12
  113.1 2.8 %collective-permute-start.13 = (bf16[2,2,256,128]{3,2,1,0:T(8,128)(2,1)S(1)}, bf16[2,2,256,128]{3,2,1,0:T(8,128)(2,1)S(1)}, u32[]{:S(2)}, u32[]{:S(2)}) collective-permute-start(bf16[2,2,256,128]{3,2,1,0:T(8,128)(2,1)S(1)} %add.47), channel_id=1, source_target_pairs={{0,253},{1,254},{2,255},{3,0},{4,1},{5,2},{6,3},{7,4},{8,5},{9,6},... | collective-permute-start | bytes 786440 | tf_op jit(solution)/shard_map/ppermute | solution.py:26
  115.9 0.7 copy-done.4
  116.6 10.1 %attend.7 = (bf16[256,4096]{1,0:T(8,128)(2,1)}, bf16[256,4096]{1,0:T(8,128)(2,1)}, f32[2,2,256,128]{3,2,1,0:T(8,128)}, bf16[2,2,256,128]{3,2,1,0:T(8,128)(2,1)},...) custom-call(s32[256,1]{1,0:T(8,128)} %copy.18.seg_col, ...), custom_call_target="tpu_custom_call", output_to_operand_aliasing={{0}: (12, {}), {1}: (13, {})} | custom-call | flops 3221225472 | bytes 8388608 | tf_op jit(solution)/shard_map/attend/pallas_call | solution.py:146
  126.8 2.3 %collective-permute-start.17 = (bf16[2,2,256,128]{3,2,1,0:T(8,128)(2,1)}, bf16[2,2,256,128]{3,2,1,0:T(8,128)(2,1)S(1)}, u32[]{:S(2)}, u32[]{:S(2)}) collective-permute-start(bf16[2,2,256,128]{3,2,1,0:T(8,128)(2,1)} %get-tuple-element.60), channel_id=1, source_target_pairs={{0,255},{1,0},{2,1},{3,2},{4,3},{5,4},{6,5},{7,6},{8,7},{9,8},{10,... | collective-permute-start | bytes 786440 | tf_op jit(solution)/shard_map/ppermute | solution.py:26
  129.9 4.4 %collective-permute-start.16 = (bf16[2,2,256,128]{3,2,1,0:T(8,128)(2,1)S(1)}, bf16[2,2,256,128]{3,2,1,0:T(8,128)(2,1)S(1)}, u32[]{:S(2)}, u32[]{:S(2)}) collective-permute-start(bf16[2,2,256,128]{3,2,1,0:T(8,128)(2,1)S(1)} %add.53), channel_id=1, source_target_pairs={{0,255},{1,0},{2,1},{3,2},{4,3},{5,4},{6,5},{7,6},{8,7},{9,8},{10,... | collective-permute-start | bytes 786440 | tf_op jit(solution)/shard_map/ppermute | solution.py:26
  134.3 3.9 %collective-permute-done.12 = bf16[2,2,256,128]{3,2,1,0:T(8,128)(2,1)S(1)} collective-permute-done((bf16[2,2,256,128]{3,2,1,0:T(8,128)(2,1)S(1)}, bf16[2,2,256,128]{3,2,1,0:T(8,128)(2,1)S(1)}, u32[]{:S(2)}, u32[]{:S(2)}) %collective-permute-start.12) | collective-permute-done | bytes 262176 | tf_op jit(solution)/shard_map/ppermute | solution.py:26
  138.4 9.3 %collective-permute-done.18 = bf16[2,2,256,128]{3,2,1,0:T(8,128)(2,1)S(1)} collective-permute-done((bf16[2,2,256,128]{3,2,1,0:T(8,128)(2,1)}, bf16[2,2,256,128]{3,2,1,0:T(8,128)(2,1)S(1)}, u32[]{:S(2)}, u32[]{:S(2)}) %collective-permute-start.18) | collective-permute-done | bytes 262176 | tf_op jit(solution)/shard_map/ppermute | solution.py:26
  147.7 6.9 %collective-permute-done.17 = bf16[2,2,256,128]{3,2,1,0:T(8,128)(2,1)S(1)} collective-permute-done((bf16[2,2,256,128]{3,2,1,0:T(8,128)(2,1)}, bf16[2,2,256,128]{3,2,1,0:T(8,128)(2,1)S(1)}, u32[]{:S(2)}, u32[]{:S(2)}) %collective-permute-start.17) | collective-permute-done | bytes 262176 | tf_op jit(solution)/shard_map/ppermute | solution.py:26
  154.9 5.6 %collective-permute-done.16 = bf16[2,2,256,128]{3,2,1,0:T(8,128)(2,1)S(1)} collective-permute-done((bf16[2,2,256,128]{3,2,1,0:T(8,128)(2,1)S(1)}, bf16[2,2,256,128]{3,2,1,0:T(8,128)(2,1)S(1)}, u32[]{:S(2)}, u32[]{:S(2)}) %collective-permute-start.16) | collective-permute-done | bytes 262176 | tf_op jit(solution)/shard_map/ppermute | solution.py:26
  160.8 6.9 %collective-permute-done.19 = bf16[2,2,256,128]{3,2,1,0:T(8,128)(2,1)S(1)} collective-permute-done((bf16[2,2,256,128]{3,2,1,0:T(8,128)(2,1)S(1)}, bf16[2,2,256,128]{3,2,1,0:T(8,128)(2,1)S(1)}, u32[]{:S(2)}, u32[]{:S(2)}) %collective-permute-start.19) | collective-permute-done | bytes 262176 | tf_op jit(solution)/shard_map/ppermute | solution.py:26
  168.0 0.7 copy-done.17
  (79 shorter events, 2.8 us)
Async XLA Ops:
  0.6 47.8 %copy-start.15 = (s32[65536]{0:T(1024)S(1)}, s32[65536]{0:T(1024)}, u32[]{:S(2)}) copy-start(s32[65536]{0:T(1024)} %param.9) | copy-start | bytes 786436
  2.0 44.8 %collective-permute-start.2 = (bf16[2,256,512]{2,1,0:T(8,128)(2,1)S(1)}, bf16[2,256,512]{2,1,0:T(8,128)(2,1)S(1)}, u32[]{:S(2)}, u32[]{:S(2)}) collective-permute-start(bf16[2,256,512]{2,1,0:T(8,128)(2,1)S(1)} %pad_maximum_fusion.1), channel_id=1, source_target_pairs={{0,1},{1,2},{2,3},{3,4},{4,5},{5,6},{6,7},{7,8},{8,9},{9,10},{10,1... | collective-permute-start | bytes 1572872 | tf_op jit(solution)/shard_map/ppermute | solution.py:26
  5.4 43.9 %collective-permute-start.1 = (bf16[2,256,512]{2,1,0:T(8,128)(2,1)S(1)}, bf16[2,256,512]{2,1,0:T(8,128)(2,1)S(1)}, u32[]{:S(2)}, u32[]{:S(2)}) collective-permute-start(bf16[2,256,512]{2,1,0:T(8,128)(2,1)S(1)} %pad_maximum_fusion), channel_id=1, source_target_pairs={{0,3},{1,4},{2,5},{3,6},{4,7},{5,8},{6,9},{7,10},{8,11},{9,12},{10... | collective-permute-start | bytes 1572872 | tf_op jit(solution)/shard_map/ppermute | solution.py:26
  7.6 51.7 %collective-permute-start = (bf16[2,256,512]{2,1,0:T(8,128)(2,1)S(1)}, bf16[2,256,512]{2,1,0:T(8,128)(2,1)S(1)}, u32[]{:S(2)}, u32[]{:S(2)}) collective-permute-start(bf16[2,256,512]{2,1,0:T(8,128)(2,1)S(1)} %pad_maximum_fusion), channel_id=1, source_target_pairs={{0,1},{1,2},{2,3},{3,4},{4,5},{5,6},{6,7},{7,8},{8,9},{9,10},{10,1... | collective-permute-start | bytes 1572872 | tf_op jit(solution)/shard_map/ppermute | solution.py:26
  9.4 50.0 %collective-permute-start.4 = (bf16[2,256,512]{2,1,0:T(8,128)(2,1)S(1)}, bf16[2,256,512]{2,1,0:T(8,128)(2,1)S(1)}, u32[]{:S(2)}, u32[]{:S(2)}) collective-permute-start(bf16[2,256,512]{2,1,0:T(8,128)(2,1)S(1)} %pad_maximum_fusion.1), channel_id=1, source_target_pairs={{0,3},{1,4},{2,5},{3,6},{4,7},{5,8},{6,9},{7,10},{8,11},{9,12},{10... | collective-permute-start | bytes 1572872 | tf_op jit(solution)/shard_map/ppermute | solution.py:26
  46.8 18.1 %copy-start.2 = (bf16[2,256,512]{2,1,0:T(8,128)(2,1)}, bf16[2,256,512]{2,1,0:T(8,128)(2,1)S(1)}, u32[]{:S(2)}) copy-start(bf16[2,256,512]{2,1,0:T(8,128)(2,1)S(1)} %collective-permute-done.2.refs_2_.refs_3_) | copy-start | bytes 1572868
  47.5 17.3 %collective-permute-start.3 = (bf16[2,256,256]{2,1,0:T(8,128)(2,1)}, bf16[2,256,256]{2,1,0:T(8,128)(2,1)}, u32[]{:S(2)}, u32[]{:S(2)}) collective-permute-start(bf16[2,256,256]{2,1,0:T(8,128)(2,1)} %slice.100), channel_id=1, source_target_pairs={{0,1},{1,2},{2,3},{3,4},{4,5},{5,6},{6,7},{7,8},{8,9},{9,10},{10,1... | collective-permute-start | bytes 786440 | tf_op jit(solution)/shard_map/ppermute | solution.py:26
  48.5 16.3 %copy-start.16 = (s32[1024]{0:T(1024)}, s32[1024]{0:T(1024)S(1)}, u32[]{:S(2)}) copy-start(s32[1024]{0:T(1024)S(1)} %pad_dynamic-slice_fusion) | copy-start | bytes 12292
  49.3 25.6 %copy-start = (bf16[2,256,512]{2,1,0:T(8,128)(2,1)}, bf16[2,256,512]{2,1,0:T(8,128)(2,1)S(1)}, u32[]{:S(2)}) copy-start(bf16[2,256,512]{2,1,0:T(8,128)(2,1)S(1)} %collective-permute-done.1.refs_6_.refs_7_) | copy-start | bytes 1572868
  49.4 66.5 %collective-permute-start.10 = (bf16[2,256,256]{2,1,0:T(8,128)(2,1)S(1)}, bf16[2,256,256]{2,1,0:T(8,128)(2,1)S(1)}, u32[]{:S(2)}, u32[]{:S(2)}) collective-permute-start(bf16[2,256,256]{2,1,0:T(8,128)(2,1)S(1)} %slice.102), channel_id=1, source_target_pairs={{0,255},{1,0},{2,1},{3,2},{4,3},{5,4},{6,5},{7,6},{8,7},{9,8},{10,... | collective-permute-start | bytes 786440 | tf_op jit(solution)/shard_map/ppermute | solution.py:26
  59.3 15.6 %copy-start.1 = (bf16[2,256,512]{2,1,0:T(8,128)(2,1)}, bf16[2,256,512]{2,1,0:T(8,128)(2,1)S(1)}, u32[]{:S(2)}) copy-start(bf16[2,256,512]{2,1,0:T(8,128)(2,1)S(1)} %collective-permute-done.refs_2_.refs_3_) | copy-start | bytes 1572868
  59.4 32.8 %collective-permute-start.11 = (bf16[2,256,256]{2,1,0:T(8,128)(2,1)S(1)}, bf16[2,256,256]{2,1,0:T(8,128)(2,1)S(1)}, u32[]{:S(2)}, u32[]{:S(2)}) collective-permute-start(bf16[2,256,256]{2,1,0:T(8,128)(2,1)S(1)} %slice.103), channel_id=1, source_target_pairs={{0,1},{1,2},{2,3},{3,4},{4,5},{5,6},{6,7},{7,8},{8,9},{9,10},{10,1... | collective-permute-start | bytes 786440 | tf_op jit(solution)/shard_map/ppermute | solution.py:26
  59.5 21.7 %collective-permute-start.7 = (bf16[2,256,256]{2,1,0:T(8,128)(2,1)S(1)}, bf16[2,256,256]{2,1,0:T(8,128)(2,1)S(1)}, u32[]{:S(2)}, u32[]{:S(2)}) collective-permute-start(bf16[2,256,256]{2,1,0:T(8,128)(2,1)S(1)} %slice.101), channel_id=1, source_target_pairs={{0,255},{1,0},{2,1},{3,2},{4,3},{5,4},{6,5},{7,6},{8,7},{9,8},{10,... | collective-permute-start | bytes 786440 | tf_op jit(solution)/shard_map/ppermute | solution.py:26
  74.9 34.3 %collective-permute-start.5 = (bf16[2,2,256,128]{3,2,1,0:T(8,128)(2,1)}, bf16[2,2,256,128]{3,2,1,0:T(8,128)(2,1)S(1)}, u32[]{:S(2)}, u32[]{:S(2)}) collective-permute-start(bf16[2,2,256,128]{3,2,1,0:T(8,128)(2,1)} %get-tuple-element.36), channel_id=1, source_target_pairs={{0,255},{1,0},{2,1},{3,2},{4,3},{5,4},{6,5},{7,6},{8,7},{9,8},{10,... | collective-permute-start | bytes 786440 | tf_op jit(solution)/shard_map/ppermute | solution.py:26
  77.5 32.0 %collective-permute-start.6 = (bf16[2,2,256,128]{3,2,1,0:T(8,128)(2,1)}, bf16[2,2,256,128]{3,2,1,0:T(8,128)(2,1)S(1)}, u32[]{:S(2)}, u32[]{:S(2)}) collective-permute-start(bf16[2,2,256,128]{3,2,1,0:T(8,128)(2,1)} %get-tuple-element.37), channel_id=1, source_target_pairs={{0,253},{1,254},{2,255},{3,0},{4,1},{5,2},{6,3},{7,4},{8,5},{9,6},... | collective-permute-start | bytes 786440 | tf_op jit(solution)/shard_map/ppermute | solution.py:26
  91.9 20.4 %collective-permute-start.8 = (bf16[2,2,256,128]{3,2,1,0:T(8,128)(2,1)}, bf16[2,2,256,128]{3,2,1,0:T(8,128)(2,1)S(1)}, u32[]{:S(2)}, u32[]{:S(2)}) collective-permute-start(bf16[2,2,256,128]{3,2,1,0:T(8,128)(2,1)} %get-tuple-element.42), channel_id=1, source_target_pairs={{0,1},{1,2},{2,3},{3,4},{4,5},{5,6},{6,7},{7,8},{8,9},{9,10},{10,1... | collective-permute-start | bytes 786440 | tf_op jit(solution)/shard_map/ppermute | solution.py:26
  92.2 20.9 %collective-permute-start.9 = (bf16[2,2,256,128]{3,2,1,0:T(8,128)(2,1)}, bf16[2,2,256,128]{3,2,1,0:T(8,128)(2,1)S(1)}, u32[]{:S(2)}, u32[]{:S(2)}) collective-permute-start(bf16[2,2,256,128]{3,2,1,0:T(8,128)(2,1)} %get-tuple-element.43), channel_id=1, source_target_pairs={{0,255},{1,0},{2,1},{3,2},{4,3},{5,4},{6,5},{7,6},{8,7},{9,8},{10,... | collective-permute-start | bytes 786440 | tf_op jit(solution)/shard_map/ppermute | solution.py:26
  99.1 13.9 %copy-start.13 = (bf16[2,2,256,128]{3,2,1,0:T(8,128)(2,1)S(1)}, bf16[2,2,256,128]{3,2,1,0:T(8,128)(2,1)}, u32[]{:S(2)}) copy-start(bf16[2,2,256,128]{3,2,1,0:T(8,128)(2,1)} %get-tuple-element.41) | copy-start | bytes 786436
  109.2 20.7 %collective-permute-start.14 = (bf16[2,2,256,128]{3,2,1,0:T(8,128)(2,1)}, bf16[2,2,256,128]{3,2,1,0:T(8,128)(2,1)S(1)}, u32[]{:S(2)}, u32[]{:S(2)}) collective-permute-start(bf16[2,2,256,128]{3,2,1,0:T(8,128)(2,1)} %get-tuple-element.55), channel_id=1, source_target_pairs={{0,253},{1,254},{2,255},{3,0},{4,1},{5,2},{6,3},{7,4},{8,5},{9,6},... | collective-permute-start | bytes 786440 | tf_op jit(solution)/shard_map/ppermute | solution.py:26
  109.4 19.7 %collective-permute-start.15 = (bf16[2,2,256,128]{3,2,1,0:T(8,128)(2,1)}, bf16[2,2,256,128]{3,2,1,0:T(8,128)(2,1)S(1)}, u32[]{:S(2)}, u32[]{:S(2)}) collective-permute-start(bf16[2,2,256,128]{3,2,1,0:T(8,128)(2,1)} %get-tuple-element.57), channel_id=1, source_target_pairs={{0,255},{1,0},{2,1},{3,2},{4,3},{5,4},{6,5},{7,6},{8,7},{9,8},{10,... | collective-permute-start | bytes 786440 | tf_op jit(solution)/shard_map/ppermute | solution.py:26
  112.3 25.9 %collective-permute-start.12 = (bf16[2,2,256,128]{3,2,1,0:T(8,128)(2,1)S(1)}, bf16[2,2,256,128]{3,2,1,0:T(8,128)(2,1)S(1)}, u32[]{:S(2)}, u32[]{:S(2)}) collective-permute-start(bf16[2,2,256,128]{3,2,1,0:T(8,128)(2,1)S(1)} %add.46), channel_id=1, source_target_pairs={{0,255},{1,0},{2,1},{3,2},{4,3},{5,4},{6,5},{7,6},{8,7},{9,8},{10,... | collective-permute-start | bytes 786440 | tf_op jit(solution)/shard_map/ppermute | solution.py:26
  113.1 41.6 %collective-permute-start.13 = (bf16[2,2,256,128]{3,2,1,0:T(8,128)(2,1)S(1)}, bf16[2,2,256,128]{3,2,1,0:T(8,128)(2,1)S(1)}, u32[]{:S(2)}, u32[]{:S(2)}) collective-permute-start(bf16[2,2,256,128]{3,2,1,0:T(8,128)(2,1)S(1)} %add.47), channel_id=1, source_target_pairs={{0,253},{1,254},{2,255},{3,0},{4,1},{5,2},{6,3},{7,4},{8,5},{9,6},... | collective-permute-start | bytes 786440 | tf_op jit(solution)/shard_map/ppermute | solution.py:26
  116.6 13.2 %copy-start.11 = (bf16[2,2,256,128]{3,2,1,0:T(8,128)(2,1)S(1)}, bf16[2,2,256,128]{3,2,1,0:T(8,128)(2,1)}, u32[]{:S(2)}) copy-start(bf16[2,2,256,128]{3,2,1,0:T(8,128)(2,1)} %get-tuple-element.56) | copy-start | bytes 786436
  116.6 21.6 %copy-start.9 = (f32[2,2,256,128]{3,2,1,0:T(8,128)S(1)}, f32[2,2,256,128]{3,2,1,0:T(8,128)}, u32[]{:S(2)}) copy-start(f32[2,2,256,128]{3,2,1,0:T(8,128)} %get-tuple-element.52) | copy-start | bytes 1572868
  126.8 20.9 %copy-start.14 = (bf16[2,2,256,128]{3,2,1,0:T(8,128)(2,1)S(1)}, bf16[2,2,256,128]{3,2,1,0:T(8,128)(2,1)}, u32[]{:S(2)}) copy-start(bf16[2,2,256,128]{3,2,1,0:T(8,128)(2,1)} %get-tuple-element.61) | copy-start | bytes 786436
  126.8 28.0 %copy-start.7 = (f32[2,2,256,128]{3,2,1,0:T(8,128)S(1)}, f32[2,2,256,128]{3,2,1,0:T(8,128)}, u32[]{:S(2)}) copy-start(f32[2,2,256,128]{3,2,1,0:T(8,128)} %get-tuple-element.53) | copy-start | bytes 1572868
  126.8 27.9 %collective-permute-start.17 = (bf16[2,2,256,128]{3,2,1,0:T(8,128)(2,1)}, bf16[2,2,256,128]{3,2,1,0:T(8,128)(2,1)S(1)}, u32[]{:S(2)}, u32[]{:S(2)}) collective-permute-start(bf16[2,2,256,128]{3,2,1,0:T(8,128)(2,1)} %get-tuple-element.60), channel_id=1, source_target_pairs={{0,255},{1,0},{2,1},{3,2},{4,3},{5,4},{6,5},{7,6},{8,7},{9,8},{10,... | collective-permute-start | bytes 786440 | tf_op jit(solution)/shard_map/ppermute | solution.py:26
  129.1 18.5 %collective-permute-start.18 = (bf16[2,2,256,128]{3,2,1,0:T(8,128)(2,1)}, bf16[2,2,256,128]{3,2,1,0:T(8,128)(2,1)S(1)}, u32[]{:S(2)}, u32[]{:S(2)}) collective-permute-start(bf16[2,2,256,128]{3,2,1,0:T(8,128)(2,1)} %get-tuple-element.62), channel_id=1, source_target_pairs={{0,1},{1,2},{2,3},{3,4},{4,5},{5,6},{6,7},{7,8},{8,9},{9,10},{10,1... | collective-permute-start | bytes 786440 | tf_op jit(solution)/shard_map/ppermute | solution.py:26
  129.9 30.7 %collective-permute-start.16 = (bf16[2,2,256,128]{3,2,1,0:T(8,128)(2,1)S(1)}, bf16[2,2,256,128]{3,2,1,0:T(8,128)(2,1)S(1)}, u32[]{:S(2)}, u32[]{:S(2)}) collective-permute-start(bf16[2,2,256,128]{3,2,1,0:T(8,128)(2,1)S(1)} %add.53), channel_id=1, source_target_pairs={{0,255},{1,0},{2,1},{3,2},{4,3},{5,4},{6,5},{7,6},{8,7},{9,8},{10,... | collective-permute-start | bytes 786440 | tf_op jit(solution)/shard_map/ppermute | solution.py:26
  138.2 22.3 %copy-start.8 = (f32[2,2,256,128]{3,2,1,0:T(8,128)S(1)}, f32[2,2,256,128]{3,2,1,0:T(8,128)}, u32[]{:S(2)}) copy-start(f32[2,2,256,128]{3,2,1,0:T(8,128)} %get-tuple-element.54) | copy-start | bytes 1572868
  154.7 13.1 %collective-permute-start.19 = (bf16[2,2,256,128]{3,2,1,0:T(8,128)(2,1)S(1)}, bf16[2,2,256,128]{3,2,1,0:T(8,128)(2,1)S(1)}, u32[]{:S(2)}, u32[]{:S(2)}) collective-permute-start(bf16[2,2,256,128]{3,2,1,0:T(8,128)(2,1)S(1)} %add.56), channel_id=1, source_target_pairs={{0,253},{1,254},{2,255},{3,0},{4,1},{5,2},{6,3},{7,4},{8,5},{9,6},... | collective-permute-start | bytes 786440 | tf_op jit(solution)/shard_map/ppermute | solution.py:26
  154.7 13.1 %copy-start.10 = (f32[2,2,256,128]{3,2,1,0:T(8,128)S(1)}, f32[2,2,256,128]{3,2,1,0:T(8,128)}, u32[]{:S(2)}) copy-start(f32[2,2,256,128]{3,2,1,0:T(8,128)} %get-tuple-element.59) | copy-start | bytes 1572868
  (7 other events, 25.7 us)
